TPU v7x, 768 devices: a whole 4x8x12 slice. The times are simulated.
768 devices in a mesh: context: 24 (over z, core), dp: 4 (over x), tensor: 8 (over y).
Axes of the slice: x: 4, y: 8, z: 12, core: 2. Of those that a mesh axis runs over, the one named last changes fastest.
Arguments:
- query_rows: bfloat16 [4, 3072, 4096], P('dp', 'context', 'tensor'), may hold values from -6 to 6
- key_rows: bfloat16 [4, 3072, 4096], P('dp', 'context', 'tensor'), may hold values from -6 to 6
- value_rows: bfloat16 [4, 3072, 4096], P('dp', 'context', 'tensor'), may hold values from -6 to 6
- out_weight: bfloat16 [4096, 6144], P('tensor', 'dp'), may hold values from -0.125 to 0.125
- grad_out: bfloat16 [4, 3072, 6144], P('dp', 'context'), may hold values from -4 to 4
Outputs:
- attended: bfloat16 [4, 3072, 6144], P('dp', 'context', 'tensor')
- grad_query: bfloat16 [4, 3072, 4096], P('dp', 'context', 'tensor')
- grad_key: bfloat16 [4, 3072, 4096], P('dp', 'context', 'tensor')
- grad_value: bfloat16 [4, 3072, 4096], P('dp', 'context', 'tensor')
All inputs are finite; a program needn't handle non-finite values.
Results may differ from a plain program's by a relative error of at most 0.025.
Values may be sent and summed in bfloat16 or wider, within the bound.
A program may use at most 64 MiB of HBM per device.

v0:
```python
import jax
import jax.numpy as jnp
from jax import lax
from jax.sharding import Mesh
from jax.sharding import PartitionSpec as P

DH = 128
CONTEXT = ("context_0", "context_1")


def filled_with(shard, identity):
    return jnp.broadcast_to(jnp.asarray(identity, shard.dtype), shard.shape)


def entering(shard, axes, combine, identity, reverse):
    before = start = filled_with(shard, identity)
    running = shard
    for axis in reversed(axes):
        devices, place = (lax.axis_size(axis), lax.axis_index(axis))
        pieces = lax.all_gather(running.astype(jnp.bfloat16), axis)
        inside, running = (start, start)
        for k in reversed(range(devices)) if reverse else range(devices):
            passed = k > place if reverse else k < place
            running = combine(running, pieces[k].astype(shard.dtype))
            inside = jnp.where(passed, running, inside)
        before = combine(inside, before)
    return before


def split_up(shard, dim, devices):
    shape = shard.shape
    tiles = shard.reshape(*shape[:dim], devices, shape[dim] // devices, *shape[dim + 1 :])
    return jnp.moveaxis(tiles, dim, 0)


def summed_on_arrival(shard, axis, dim):
    tiles = split_up(shard, dim, lax.axis_size(axis))
    arrived = lax.all_to_all(tiles, axis, split_axis=0, concat_axis=0, tiled=True)
    return arrived.astype(jnp.float32).sum(axis=0)


def add_states(earlier, later):
    return earlier + later


def shards(query_rows, key_rows, value_rows, out_weight, grad_out):
    seq_rows = query_rows.shape[1]
    head_width = query_rows.shape[2]
    heads_here = head_width // DH
    factor = float(DH * seq_rows * lax.axis_size(CONTEXT)) ** (-0.5)
    places = jnp.arange(seq_rows)
    causal = (places[:, None] >= places[None, :]).astype(jnp.float32)
    panel = lax.all_gather(out_weight, "dp", axis=1, tiled=True)
    grad_attn = jnp.einsum(
        "rm,hm->rh", grad_out[0], panel, preferred_element_type=jnp.float32
    ).astype(jnp.bfloat16)

    def heads_of(array):
        return array.reshape(seq_rows, heads_here, DH)

    q_half = heads_of(query_rows[0])
    k_half = heads_of(key_rows[0])
    v_half = heads_of(value_rows[0])
    g_half = heads_of(grad_attn)
    local_kv = jnp.einsum("chd,che->hde", k_half, v_half, preferred_element_type=jnp.float32)
    local_qd = jnp.einsum("bhd,bhe->hde", q_half, g_half, preferred_element_type=jnp.float32)
    zero_state = jnp.zeros_like(local_kv)
    prefix = entering(local_kv, CONTEXT, add_states, zero_state, False)
    suffix = entering(local_qd, CONTEXT, add_states, zero_state, True)
    scores = jnp.einsum("bhd,chd->hbc", q_half, k_half, preferred_element_type=jnp.float32) * causal
    d_scores = (
        jnp.einsum("bhe,che->hbc", g_half, v_half, preferred_element_type=jnp.float32) * causal
    )
    queries = q_half.astype(jnp.float32)
    key_vals = k_half.astype(jnp.float32)
    val_vals = v_half.astype(jnp.float32)
    grads = g_half.astype(jnp.float32)
    attn_out = factor * (
        jnp.einsum("hbc,che->bhe", scores, val_vals) + jnp.einsum("bhd,hde->bhe", queries, prefix)
    )
    grad_q = factor * (
        jnp.einsum("hbc,chd->bhd", d_scores, key_vals) + jnp.einsum("bhe,hde->bhd", grads, prefix)
    )
    grad_k = factor * (
        jnp.einsum("hbc,bhd->chd", d_scores, queries) + jnp.einsum("che,hde->chd", val_vals, suffix)
    )
    grad_v = factor * (
        jnp.einsum("hbc,bhe->che", scores, grads) + jnp.einsum("chd,hde->che", key_vals, suffix)
    )
    attn_flat = attn_out.reshape(seq_rows, head_width).astype(jnp.bfloat16)
    summed = summed_on_arrival(
        jnp.einsum("hm,rh->mr", panel, attn_flat, preferred_element_type=jnp.float32).astype(
            jnp.bfloat16
        ),
        "tensor",
        0,
    )
    attended = summed.T.astype(jnp.bfloat16)[None]

    def packed(array):
        return array.reshape(1, seq_rows, head_width).astype(jnp.bfloat16)

    return (attended, packed(grad_q), packed(grad_k), packed(grad_v))


def solution(mesh):
    split = Mesh(
        mesh.devices.reshape(12, 2, mesh.shape["dp"], mesh.shape["tensor"]),
        ("context_0", "context_1", "dp", "tensor"),
    )
    in_specs = (
        P("dp", CONTEXT, "tensor"),
        P("dp", CONTEXT, "tensor"),
        P("dp", CONTEXT, "tensor"),
        P("tensor", "dp"),
        P("dp", CONTEXT, None),
    )
    out_specs = (
        P("dp", CONTEXT, "tensor"),
        P("dp", CONTEXT, "tensor"),
        P("dp", CONTEXT, "tensor"),
        P("dp", CONTEXT, "tensor"),
    )
    return jax.shard_map(
        shards, mesh=split, in_specs=in_specs, out_specs=out_specs, check_vma=False
    )
```

profile of v0, /device:TPU:6, one launch (start us, length us, event | category | flops | bytes accessed | tf_op | source)
XLA Modules:
  0.0 234.1 jit_solution(11293329249738950708)
XLA Ops:
  7.2 0.0 copy-start
  7.2 0.0 all-gather.6.cloned.1.call-start
  7.2 1.0 reshape_squeeze.11
  8.3 0.9 reshape_squeeze.10
  9.2 0.0 copy-start.12
  9.2 0.1 copy.34
  9.4 0.6 copy-done.6
  10.0 0.2 convolution_convert_fusion.2
  10.2 2.0 all-gather
  12.2 0.7 fusion.47
  12.9 0.0 all-gather.6.cloned.1.call-update
  12.9 0.0 all-gather.8.cloned.1.call-start
  13.0 0.7 all-gather.8.cloned.1.call-update
  13.7 0.0 all-gather.10.cloned.1.call-start
  13.9 0.0 copy-start.11
  13.9 0.6 copy-done.11
  14.5 0.2 convolution_multiply_fusion.1
  14.7 0.2 convolution_bitcast_fusion.5
  14.9 65.2 %all-gather.6.cloned.1.call-done = bf16[12,4,128,128]{3,2,1,0:T(8,128)(2,1)} async-done(((bf16[1,4,128,128]{3,2,1,0:T(8,128)(2,1)}), bf16[12,4,128,128]{3,2,1,0:T(8,128)(2,1)}) %all-gather.6.cloned.1.call-update) | async-done | bytes 1572880 | tf_op jit(solution)/shard_map/all_gather | solution.py:20
  80.2 1.8 fusion.29
  82.0 0.2 fusion.9
  82.2 69.5 %all-gather.8.cloned.1.call-done = bf16[512,6144]{1,0:T(8,128)(2,1)} async-done(((bf16[512,1536]{1,0:T(8,128)(2,1)}), bf16[512,6144]{1,0:T(8,128)(2,1)}) %all-gather.8.cloned.1.call-update) | async-done | bytes 6291472 | tf_op jit(solution)/shard_map/all_gather | solution.py:53
  151.8 5.0 %fusion.13 = bf16[128,512]{1,0:T(8,128)(2,1)S(1)} fusion(bf16[512,6144]{1,0:T(8,128)(2,1)} %all-gather.8.cloned.1.call-done, bf16[1,128,6144]{2,1,0:T(8,128)(2,1)S(1)} %copy-done), kind=kOutput, calls=%fused_computation.26 | convolution fusion | flops 805371904 | bytes 7995392 | tf_op jit(solution)/shard_map/rm,hm->rh/dot_general | solution.py:54
  156.8 0.1 copy.56
  156.9 0.2 fusion.16
  157.1 0.1 copy.46
  157.3 2.0 all-gather.1
  159.3 0.8 copy-done.1
  160.0 0.7 fusion.48
  160.7 0.0 all-gather.10.cloned.1.call-update
  160.7 3.8 %convolution_convert_fusion = bf16[128,6144]{1,0:T(8,128)(2,1)S(1)} fusion(bf16[128,512]{0,1:T(8,128)(2,1)S(1)} %bitcast.87, bf16[512,6144]{1,0:T(8,128)(2,1)} %all-gather.8.cloned.1.call-done), kind=kOutput, calls=%fused_computation | convolution fusion | flops 806092800 | bytes 7995392 | tf_op jit(solution)/shard_map/hm,rh->mr/dot_general | solution.py:92
  164.5 1.3 copy.79
  165.8 7.0 %all-to-all-start = ((bf16[8,768,128]{1,2,0:T(8,128)(2,1)}), bf16[8,768,128]{1,2,0:T(8,128)(2,1)S(1)}, u32[]{:S(2)}, u32[]{:S(2)}) async-start(bf16[8,768,128]{1,2,0:T(8,128)(2,1)} %bitcast.81), calls=%async_computation | async-start | bytes 3145728 | tf_op jit(solution)/shard_map/all_to_all | solution.py:38
  172.8 1.1 convolution_multiply_fusion
  173.9 0.6 copy-done.8
  174.5 1.1 convolution_bitcast_fusion.3
  175.7 1.7 fusion.10
  177.4 1.7 copy.51
  179.1 1.8 convolution_bitcast_fusion.1
  180.9 1.8 fusion.60
  182.7 30.4 %all-to-all-done = bf16[8,768,128]{1,2,0:T(8,128)(2,1)S(1)} async-done(((bf16[8,768,128]{1,2,0:T(8,128)(2,1)}), bf16[8,768,128]{1,2,0:T(8,128)(2,1)S(1)}, u32[]{:S(2)}, u32[]{:S(2)}) %all-to-all-start) | async-done | bytes 1572896 | tf_op jit(solution)/shard_map/all_to_all | solution.py:38
  213.1 0.9 reduce_sum.12
  214.0 9.7 %all-gather.10.cloned.1.call-done = bf16[12,4,128,128]{3,2,1,0:T(8,128)(2,1)} async-done(((bf16[1,4,128,128]{3,2,1,0:T(8,128)(2,1)}), bf16[12,4,128,128]{3,2,1,0:T(8,128)(2,1)}) %all-gather.10.cloned.1.call-update) | async-done | bytes 1572880 | tf_op jit(solution)/shard_map/all_gather | solution.py:20
  223.7 1.8 fusion.42
  225.5 0.2 fusion.11
  225.8 0.8 copy.52
  226.5 0.2 fusion.12
  226.8 0.8 copy.53
  (21 shorter events, 0.1 us)
Async XLA Ops:
  7.2 144.6 %copy-start = (bf16[1,128,6144]{2,1,0:T(8,128)(2,1)S(1)}, bf16[1,128,6144]{2,1,0:T(8,128)(2,1)}, u32[]{:S(2)}) copy-start(bf16[1,128,6144]{2,1,0:T(8,128)(2,1)} %param.9) | copy-start | bytes 4718596
  7.2 73.0 %all-gather.6.cloned.1.call-start = ((), (), s32[]{:S(2)}) async-start(), calls=%async_computation.1 | async-start | bytes 1703936 | tf_op jit(solution)/shard_map/all_gather | solution.py:20
  9.2 4.6 %copy-start.3 = (bf16[128,4,128]{2,1,0:T(4,128)(2,1)}, bf16[128,4,128]{2,1,0:T(4,128)(2,1)S(1)}, u32[]{:S(2)}) copy-start(bf16[128,4,128]{2,1,0:T(4,128)(2,1)S(1)} %reshape_squeeze.10) | copy-start | bytes 393220
  9.2 4.5 %copy-start.12 = (bf16[1,128,512]{2,1,0:T(8,128)(2,1)S(1)}, bf16[1,128,512]{2,1,0:T(8,128)(2,1)}, u32[]{:S(2)}) copy-start(bf16[1,128,512]{2,1,0:T(8,128)(2,1)} %param.5) | copy-start | bytes 393220
  9.4 0.7 copy-start.6
  12.9 138.9 %all-gather.8.cloned.1.call-start = ((), (), s32[]{:S(2)}) async-start(), calls=%async_computation.2 | async-start | bytes 7864320 | tf_op jit(solution)/shard_map/all_gather | solution.py:53
  13.7 210.0 %all-gather.10.cloned.1.call-start = ((), (), s32[]{:S(2)}) async-start(), calls=%async_computation.3 | async-start | bytes 1703936 | tf_op jit(solution)/shard_map/all_gather | solution.py:20
  13.9 0.6 copy-start.11
  14.7 67.5 %copy-start.7 = (bf16[4,128,128]{2,1,0:T(8,128)(2,1)}, bf16[4,128,128]{2,1,0:T(8,128)(2,1)S(1)}, u32[]{:S(2)}) copy-start(bf16[4,128,128]{2,1,0:T(8,128)(2,1)S(1)} %convolution_multiply_fusion.1) | copy-start | bytes 393220
  82.0 74.8 %copy-start.5 = (bf16[4,128,128]{2,1,0:T(8,128)(2,1)}, bf16[4,128,128]{2,1,0:T(8,128)(2,1)S(1)}, u32[]{:S(2)}) copy-start(bf16[4,128,128]{2,1,0:T(8,128)(2,1)S(1)} %fusion.29) | copy-start | bytes 393220
  159.3 0.8 copy-start.1
  165.8 47.3 %all-to-all-start = ((bf16[8,768,128]{1,2,0:T(8,128)(2,1)}), bf16[8,768,128]{1,2,0:T(8,128)(2,1)S(1)}, u32[]{:S(2)}, u32[]{:S(2)}) async-start(bf16[8,768,128]{1,2,0:T(8,128)(2,1)} %bitcast.81), calls=%async_computation | async-start | bytes 3145728 | tf_op jit(solution)/shard_map/all_to_all | solution.py:38
  173.9 0.7 copy-start.8
  182.7 41.0 %copy-start.2 = (bf16[8,128,128]{2,1,0:T(8,128)(2,1)S(1)}, bf16[8,128,128]{2,1,0:T(8,128)(2,1)}, u32[]{:S(2)}) copy-start(bf16[8,128,128]{2,1,0:T(8,128)(2,1)} %copy-done.1) | copy-start | bytes 786436
  214.0 11.5 %copy-start.10 = (f32[128,4,128]{0,2,1:T(8,128)S(1)}, f32[128,4,128]{0,2,1:T(8,128)}, u32[]{:S(2)}) copy-start(f32[128,4,128]{0,2,1:T(8,128)} %convolution_bitcast_fusion.1) | copy-start | bytes 786436
  214.0 12.5 %copy-start.4 = (bf16[128,4,128]{2,1,0:T(4,128)(2,1)S(1)}, bf16[128,4,128]{2,1,0:T(4,128)(2,1)}, u32[]{:S(2)}) copy-start(bf16[128,4,128]{2,1,0:T(4,128)(2,1)} %copy-done.3) | copy-start | bytes 393220
  214.0 12.5 %copy-start.9 = (f32[4,128,128]{2,1,0:T(8,128)S(1)}, f32[4,128,128]{2,1,0:T(8,128)}, u32[]{:S(2)}) copy-start(f32[4,128,128]{2,1,0:T(8,128)} %fusion.60) | copy-start | bytes 786436
Sparse Core Ops, SparseCore 0:
  13.1 67.0 all-gather.5
  82.5 69.2 all-gather.7
  160.9 62.8 all-gather.9
where the time goes:
time: 235 us; the launch traced here: 234 us
  waiting for transfers between devices  176 us (75%)
  matrix products  17.8 us (8%)
  between operations  14 us (6%)
  local copies, waits for them, and re-layouts  9.62 us (4%)
  starting transfers between devices  7.1 us (3%)
  other arithmetic  5.94 us (3%)
  blocking collectives  3.99 us (2%)
    all_gather x2, waiting for transfers between devices, entering(): pieces = lax.all_gather(running.astype(jnp.bfloat16), axis)  74.9 us
    all_gather x1, waiting for transfers between devices, shards(): panel = lax.all_gather(out_weight, 'dp', axis=1, tiled=True)  69.5 us
    all_to_all x1, waiting for transfers between devices, summed_on_arrival(): lax.all_to_all(tiles, axis, split_axis=0, concat_axis=0, tiled=True)  30.4 us
    all_to_all x1, starting transfers between devices, summed_on_arrival(): lax.all_to_all(tiles, axis, split_axis=0, concat_axis=0, tiled=True)  6.98 us
    unnamed x29, local copies, waits for them, and re-layouts  5.93 us
    dot_general x1, matrix products, shards(): jnp.einsum('rm,hm->rh', grad_out[0], panel, preferred_element_type=jnp.fl...  5.01 us
  transfers between devices with their start and end apart: 4, of which 4 were waited for; matrix products, arithmetic and copies ran while one was open for 8% of the time, Pallas kernels for 0%

commit v1 on v0

v1 whole, which is shorter than its diff:
```python
import functools

import jax
import jax.numpy as jnp
from jax import lax
from jax.experimental import pallas as pl
from jax.experimental.pallas import tpu as pltpu
from jax.sharding import PartitionSpec as P

DH = 128
BF = jnp.bfloat16
F32 = jnp.float32
MESH = pl.DeviceIdType.MESH


def dot(a, b, ca, cb):
    return lax.dot_general(a, b, (((ca,), (cb,)), ((), ())), preferred_element_type=F32)


def kernel(
    sizes, q_hbm, k_hbm, v_hbm, w_hbm, go_hbm, att_ref, dq_ref, dk_ref, dv_ref,
    q_ref, k_ref, v_ref, panel, go, grad_acc, attn32, attn16, part, y_in,
    local_kv, local_qd, got_kv, got_qd, tot_kv, tot_qd, far_kv, far_qd,
    out_kv, out_qd, prefix, suffix, send_sem, recv_sem, load_sem,
):
    n_ctx, n_x, n_y, factor = sizes
    rows, width = q_ref.shape
    heads = width // DH
    wide = panel.shape[2]
    c, x, y = lax.axis_index("context"), lax.axis_index("dp"), lax.axis_index("tensor")
    core, z = lax.rem(c, 2), c // 2
    parity = lax.rem(z, 2)
    member, group = lax.rem(c, 8), c // 8
    n_groups = n_ctx // 8

    def at_ctx(i):
        return {"context": lax.rem(i + n_ctx, n_ctx)}

    right_x, left_x = {"dp": lax.rem(x + 1, n_x)}, {"dp": lax.rem(x + n_x - 1, n_x)}
    up_y, down_y = {"tensor": lax.rem(y + 1, n_y)}, {"tensor": lax.rem(y + n_y - 1, n_y)}
    up_z, down_z = at_ctx(c + 2), at_ctx(c - 2)
    sibling = {"context": c + 1 - 2 * core}

    def mate(i):
        return {"context": c - member + i}

    barrier = pltpu.get_barrier_semaphore()
    peers = [right_x, left_x, up_y, down_y, up_z, down_z]
    peers += [mate(lax.rem(member + o, 8)) for o in range(1, 8)]
    peers += [at_ctx(c + 8 * o) for o in range(1, n_groups)]
    for peer in peers:
        pl.semaphore_signal(barrier, inc=1, device_id=peer, device_id_type=MESH)

    loads = []

    def load(src, dst):
        copy = pltpu.make_async_copy(src, dst, load_sem.at[len(loads)])
        copy.start()
        loads.append(copy)
        return copy

    load_k = load(k_hbm.at[0], k_ref)
    load_v = load(v_hbm.at[0], v_ref)
    load_q = load(q_hbm.at[0], q_ref)
    load_w = load(w_hbm, panel.at[0])
    load_go = []
    for r in range(n_x):
        columns = pl.ds(pl.multiple_of(lax.rem(x + r, n_x) * wide, wide), wide)
        load_go.append(load(go_hbm.at[0, :, columns], go.at[r]))
    pl.semaphore_wait(barrier, len(peers))

    sent = []

    def send(src, dst, here, device):
        i = len(sent)
        copy = pltpu.make_async_remote_copy(
            src, dst, send_sem.at[i], recv_sem.at[i], device, MESH
        )
        copy.start()
        sent.append(copy)
        landing = pltpu.make_async_remote_copy(
            src, here, send_sem.at[i], recv_sem.at[i], device, MESH
        )
        return landing.wait_recv

    def piece(ref, par, cor, d):
        start = pl.multiple_of(par * 256 + cor * 128 + d * 64, 64)
        return ref.at[pl.ds(start, 64)]

    def mine(ref, d):
        return piece(ref, parity, core, d)

    def x_send(src, r, d, device):
        dst = mine(panel.at[r], d)
        return send(src, dst, dst, device)

    x_got = {}
    x_got[3, 0] = x_send(mine(w_hbm, 0), 3, 0, right_x)
    x_got[1, 1] = x_send(mine(w_hbm, 1), 1, 1, left_x)
    x_got[3, 1] = x_send(mine(w_hbm, 1), 3, 1, right_x)
    x_got[1, 0] = x_send(mine(w_hbm, 0), 1, 0, left_x)
    z_got, pass_x, pass_z = {}, {}, {}

    def on_x(r, d):
        x_got[r, d]()
        block = mine(panel.at[r], d)
        if (r, d) == (3, 0):
            x_got[2, 0] = x_send(block, 2, 0, right_x)
        if (r, d) == (1, 1):
            x_got[2, 1] = x_send(block, 2, 1, left_x)
        other = piece(panel.at[r], 1 - parity, core, d)
        z_got[r, d] = send(block, block, other, up_z if d == 0 else down_z)
        theirs = piece(panel.at[r], parity, 1 - core, d)
        pass_x[r, d] = send(block, block, theirs, sibling)

    def on_z(r, d):
        z_got[r, d]()
        block = piece(panel.at[r], 1 - parity, core, d)
        theirs = piece(panel.at[r], 1 - parity, 1 - core, d)
        pass_z[r, d] = send(block, block, theirs, sibling)

    def slot_done(r):
        for d in range(2):
            pass_x[r, d]()
            pass_z[r, d]()

    def part_of(ref, i):
        return ref.at[pl.ds(pl.multiple_of(i * 64, 64), 64)]

    def spread(local, got):
        waits = []
        for o in range(1, 8):
            to, source = lax.rem(member + o, 8), lax.rem(member + 8 - o, 8)
            waits.append(
                send(part_of(local, to), part_of(got, member), part_of(got, source), mate(to))
            )
        part_of(got, member)[...] = part_of(local, member)[...]
        return waits

    def totals(waits, got, tot, far):
        for wait in waits:
            wait()
        tot[...] = sum(got[i * 64 : i * 64 + 64].astype(F32) for i in range(8)).astype(BF)
        return [
            send(tot, far.at[o - 1], far.at[o - 1], at_ctx(c + 8 * o))
            for o in range(1, n_groups)
        ]

    def scan(waits, got, far, out, state, reverse):
        running = jnp.zeros((64, DH), F32)
        for o in range(1, n_groups):
            waits[o - 1]()
            earlier = group >= o
            keep = jnp.where(earlier, 0.0, 1.0) if reverse else jnp.where(earlier, 1.0, 0.0)
            running = running + keep.astype(F32) * far[o - 1].astype(F32)
        for i in reversed(range(8)) if reverse else range(8):
            out[i * 64 : i * 64 + 64] = running.astype(BF)
            running = running + got[i * 64 : i * 64 + 64].astype(F32)
        waits = []
        for o in range(1, 8):
            to, source = lax.rem(member + o, 8), lax.rem(member + 8 - o, 8)
            waits.append(
                send(part_of(out, to), part_of(state, member), part_of(state, source), mate(to))
            )
        part_of(state, member)[...] = part_of(out, member)[...]
        return waits

    def head(ref, h):
        return ref[:, h * DH : (h + 1) * DH]

    def state_of(ref, h):
        return ref[h * DH : (h + 1) * DH, :]

    first = lax.broadcasted_iota(jnp.int32, (rows, rows), 0)
    second = lax.broadcasted_iota(jnp.int32, (rows, rows), 1)
    causal = (first >= second).astype(F32)
    causal_t = (first <= second).astype(F32)

    load_k.wait()
    load_v.wait()
    for h in range(heads):
        local_kv[h * DH : (h + 1) * DH, :] = dot(head(k_ref, h), head(v_ref, h), 0, 0).astype(BF)
    kv_waits = spread(local_kv, got_kv)

    load_q.wait()
    for h in range(heads):
        scores = (dot(head(q_ref, h), head(k_ref, h), 1, 1) * causal).astype(BF)
        attn32[:, h * DH : (h + 1) * DH] = dot(scores, head(v_ref, h), 1, 0)

    kv_waits = totals(kv_waits, got_kv, tot_kv, far_kv)
    load_w.wait()
    load_go[0].wait()
    grad_acc[...] = dot(go[0], panel[0], 1, 1)

    kv_waits = scan(kv_waits, got_kv, far_kv, out_kv, prefix, False)
    on_x(3, 0)
    on_x(1, 1)
    for wait in kv_waits:
        wait()
    for h in range(heads):
        total = attn32[:, h * DH : (h + 1) * DH] + dot(head(q_ref, h), state_of(prefix, h), 1, 0)
        attn16[:, h * DH : (h + 1) * DH] = (factor * total).astype(BF)

    half = wide // 4

    def project(r):
        for i in range(4):
            part[r * 4 + i] = dot(
                attn16[...], panel[r, :, i * half : (i + 1) * half], 1, 0
            ).astype(BF)

    project(0)
    on_x(3, 1)
    on_x(1, 0)
    on_z(3, 0)
    on_z(1, 1)
    on_x(2, 0)
    on_x(2, 1)
    on_z(3, 1)
    on_z(1, 0)
    for r in (3, 1):
        slot_done(r)
        load_go[r].wait()
        grad_acc[...] += dot(go[r], panel[r], 1, 1)
        project(r)
    on_z(2, 0)
    on_z(2, 1)
    slot_done(2)
    load_go[2].wait()

    def chunk_of(to, which):
        slot = lax.rem(to // 2 + n_x - x, n_x)
        return slot * 4 + lax.rem(to, 2) * 2 + which

    distance = (4, 3, 3, 2, 2, 1, 1)
    y_got = ([], [])

    def y_step(j):
        for way in range(2):
            to = lax.rem(y + (distance[j] if way == 0 else n_y - distance[j]), n_y)
            chunk = chunk_of(to, (j + way) % 2)
            if j >= 2:
                y_got[way][j - 2]()
                total = part[chunk].astype(F32) + y_in[way * 7 + j - 2].astype(F32)
                part[chunk] = total.astype(BF)
            landing = y_in.at[way * 7 + j]
            y_got[way].append(
                send(part.at[chunk], landing, landing, up_y if way == 0 else down_y)
            )

    project(2)
    y_step(0)
    y_step(1)
    grads = (grad_acc[...] + dot(go[2], panel[2], 1, 1)).astype(BF)
    g_heads = [grads[:, h * DH : (h + 1) * DH] for h in range(heads)]
    for h in range(heads):
        local_qd[h * DH : (h + 1) * DH, :] = dot(head(q_ref, h), g_heads[h], 0, 0).astype(BF)
    qd_waits = spread(local_qd, got_qd)
    y_step(2)
    qd_waits = totals(qd_waits, got_qd, tot_qd, far_qd)
    y_step(3)
    for h in range(heads):
        own = slice(h * DH, (h + 1) * DH)
        d_scores = (dot(g_heads[h], head(v_ref, h), 1, 1) * causal).astype(BF)
        total = dot(d_scores, head(k_ref, h), 1, 0) + dot(g_heads[h], state_of(prefix, h), 1, 1)
        dq_ref[0, :, own] = (factor * total).astype(BF)
    qd_waits = scan(qd_waits, got_qd, far_qd, out_qd, suffix, True)
    y_step(4)
    for wait in qd_waits:
        wait()
    for h in range(heads):
        own = slice(h * DH, (h + 1) * DH)
        d_scores = (dot(head(v_ref, h), g_heads[h], 1, 1) * causal_t).astype(BF)
        total = dot(d_scores, head(q_ref, h), 1, 0) + dot(head(v_ref, h), state_of(suffix, h), 1, 1)
        dk_ref[0, :, own] = (factor * total).astype(BF)
        scores = (dot(head(k_ref, h), head(q_ref, h), 1, 1) * causal_t).astype(BF)
        total = dot(scores, g_heads[h], 1, 0) + dot(head(k_ref, h), state_of(suffix, h), 1, 0)
        dv_ref[0, :, own] = (factor * total).astype(BF)
    y_step(5)
    y_step(6)
    for which in range(2):
        up, down = 6 - which, 5 + which
        y_got[0][up]()
        y_got[1][down]()
        total = part[chunk_of(y, which)].astype(F32)
        total = total + y_in[up].astype(F32) + y_in[7 + down].astype(F32)
        att_ref[0, :, which * half : (which + 1) * half] = total.astype(BF)
    for copy in sent:
        copy.wait_send()


def solution(mesh):
    n_ctx, n_x, n_y = mesh.shape["context"], mesh.shape["dp"], mesh.shape["tensor"]

    def shards(q, k, v, w, go):
        _, rows, width = q.shape
        depth, wide = w.shape
        factor = float(DH * rows * n_ctx) ** (-0.5)
        states = width // DH * DH
        half = wide // 4
        sizes = (n_ctx, n_x, n_y, factor)
        head_out = jax.ShapeDtypeStruct((1, rows, width), BF)
        state = pltpu.VMEM((states, DH), BF)
        total = pltpu.VMEM((states // 8, DH), BF)
        far = pltpu.VMEM((2, states // 8, DH), BF)
        return pl.pallas_call(
            functools.partial(kernel, sizes),
            out_shape=(
                jax.ShapeDtypeStruct((1, rows, n_x * wide // n_y), BF),
                head_out,
                head_out,
                head_out,
            ),
            in_specs=[pl.BlockSpec(memory_space=pl.ANY)] * 5,
            out_specs=[pl.BlockSpec(memory_space=pltpu.VMEM)] * 4,
            scratch_shapes=[
                pltpu.VMEM((rows, width), BF),
                pltpu.VMEM((rows, width), BF),
                pltpu.VMEM((rows, width), BF),
                pltpu.VMEM((n_x, depth, wide), BF),
                pltpu.VMEM((n_x, rows, wide), BF),
                pltpu.VMEM((rows, width), F32),
                pltpu.VMEM((rows, width), F32),
                pltpu.VMEM((rows, width), BF),
                pltpu.VMEM((4 * n_x, rows, half), BF),
                pltpu.VMEM((14, rows, half), BF),
                state, state, state, state, total, total, far, far,
                state, state, state, state,
                pltpu.SemaphoreType.DMA((70,)),
                pltpu.SemaphoreType.DMA((70,)),
                pltpu.SemaphoreType.DMA((8,)),
            ],
            compiler_params=pltpu.CompilerParams(
                collective_id=0, has_side_effects=True, vmem_limit_bytes=56 << 20
            ),
        )(q, k, v, w, go)

    rows_spec = P("dp", "context", "tensor")
    return jax.shard_map(
        shards,
        mesh=mesh,
        in_specs=(rows_spec, rows_spec, rows_spec, P("tensor", "dp"), P("dp", "context", None)),
        out_specs=(rows_spec,) * 4,
        check_vma=False,
    )
```

time: 235 us -> 76.9 us (0.33)
  the two profiles are of different devices: /device:TPU:6 before, /device:TPU:1 now
where the time goes in v1:
time: 76.9 us; the launch traced here: 76.7 us
  Pallas kernels  69.7 us (91%)
  local copies, waits for them, and re-layouts  6.32 us (8%)
    pallas_call x1, Pallas kernels, shards(): pl.pallas_call(functools.partial(kernel, sizes), out_shape=(jax.ShapeDtyp...  69.7 us
    unnamed x4, local copies, waits for them, and re-layouts  6.32 us

profile of v1, /device:TPU:1, one launch (start us, length us, event | category | flops | bytes accessed | tf_op | source)
XLA Modules:
  0.0 76.7 jit_solution(7857778852010522249)
XLA Ops:
  0.6 69.7 %shard_map.84 = (bf16[1,128,768]{2,1,0:T(8,128)(2,1)}, bf16[1,128,512]{2,1,0:T(8,128)(2,1)}, bf16[1,128,512]{2,1,0:T(8,128)(2,1)}, bf16[1,128,512]{2,1,0:T(8,128)(2,1)}) custom-call(bf16[1,128,512]{2,1,0:T(8,128)(2,1)} %q_hbm.1, bf16[1,128,512]{2,1,0:T(8,128)(2,1)} %k_hbm.1, bf16[1,128,512]{2,1,0:T(8,128)(2,1)} %v_hbm.1, bf16[512,1536]{1,0:T(8,128)(2,1)} %w_hbm.1, ...), custom_call_target="tpu_custom_call" | custom-call | tf_op jit(solution)/shard_map/pallas_call | solution.py:306
  70.4 1.6 %copy.13 = bf16[1,128,768]{2,1,0:T(8,128)(2,1)} copy(bf16[1,128,768]{2,1,0:T(8,128)(2,1)} %get-tuple-element.8) | data formatting | bytes 393216
  72.0 1.6 %copy.14 = bf16[1,128,512]{2,1,0:T(8,128)(2,1)} copy(bf16[1,128,512]{2,1,0:T(8,128)(2,1)} %get-tuple-element.9) | data formatting | bytes 262144
  73.6 1.6 %copy.15 = bf16[1,128,512]{2,1,0:T(8,128)(2,1)} copy(bf16[1,128,512]{2,1,0:T(8,128)(2,1)} %get-tuple-element.10) | data formatting | bytes 262144
  75.1 1.6 %copy.16 = bf16[1,128,512]{2,1,0:T(8,128)(2,1)} copy(bf16[1,128,512]{2,1,0:T(8,128)(2,1)} %get-tuple-element.11) | data formatting | bytes 262144

commit v2 on v1

--- a/solution.py
+++ b/solution.py
@@ -26,7 +26,7 @@
     n_ctx, n_x, n_y, factor = sizes
     rows, width = q_ref.shape
     heads = width // DH
-    wide = panel.shape[2]
+    depth, wide = panel.shape[1:]
     c, x, y = lax.axis_index("context"), lax.axis_index("dp"), lax.axis_index("tensor")
     core, z = lax.rem(c, 2), c // 2
     parity = lax.rem(z, 2)
@@ -83,53 +83,68 @@
         )
         return landing.wait_recv
 
-    def piece(ref, par, cor, d):
-        start = pl.multiple_of(par * 256 + cor * 128 + d * 64, 64)
-        return ref.at[pl.ds(start, 64)]
-
-    def mine(ref, d):
-        return piece(ref, parity, core, d)
-
-    def x_send(src, r, d, device):
-        dst = mine(panel.at[r], d)
-        return send(src, dst, dst, device)
-
-    x_got = {}
-    x_got[3, 0] = x_send(mine(w_hbm, 0), 3, 0, right_x)
-    x_got[1, 1] = x_send(mine(w_hbm, 1), 1, 1, left_x)
-    x_got[3, 1] = x_send(mine(w_hbm, 1), 3, 1, right_x)
-    x_got[1, 0] = x_send(mine(w_hbm, 0), 1, 0, left_x)
-    z_got, pass_x, pass_z = {}, {}, {}
-
-    def on_x(r, d):
-        x_got[r, d]()
-        block = mine(panel.at[r], d)
-        if (r, d) == (3, 0):
-            x_got[2, 0] = x_send(block, 2, 0, right_x)
-        if (r, d) == (1, 1):
-            x_got[2, 1] = x_send(block, 2, 1, left_x)
-        other = piece(panel.at[r], 1 - parity, core, d)
-        z_got[r, d] = send(block, block, other, up_z if d == 0 else down_z)
-        theirs = piece(panel.at[r], parity, 1 - core, d)
-        pass_x[r, d] = send(block, block, theirs, sibling)
+    share = depth * 3 // 32
+    rest = depth // 16
+
+    def rows_of(r, par, cor, d, at, size):
+        if par is None:
+            start = 8 * share + (cor * 2 + d) * rest
+        else:
+            start = (par * 4 + cor * 2 + d) * share
+        where = pl.ds(pl.multiple_of(start + at, 16), size)
+        return w_hbm.at[where] if r == 0 else panel.at[r, where]
+
+    fine, coarse, whole = [(0, 16), (16, share - 16)], [(0, share)], [(0, rest)]
+    x_got, z_got, passed = {}, {}, [[], [], [], []]
+
+    def x_send(source, r, shared, d, at, size):
+        par = parity if shared else None
+        dst = rows_of(r, par, core, d, at, size)
+        device = right_x if r == 3 or (r == 2 and d == 0) else left_x
+        got = send(rows_of(source, par, core, d, at, size), dst, dst, device)
+        x_got.setdefault((r, shared, d), []).append((at, size, got))
+
+    def own_x(shared, d, pieces, r):
+        for at, size in pieces:
+            x_send(0, r, shared, d, at, size)
+
+    def pass_on(r, par, d, at, size):
+        block = rows_of(r, par, core, d, at, size)
+        theirs = rows_of(r, par, 1 - core, d, at, size)
+        passed[r].append(send(block, block, theirs, sibling))
+
+    def on_x(r, shared, d):
+        for at, size, got in x_got[r, shared, d]:
+            got()
+            if (r, d) == (3, 0) or (r, d) == (1, 1):
+                x_send(r, 2, shared, d, at, size)
+            if shared:
+                block = rows_of(r, parity, core, d, at, size)
+                other = rows_of(r, 1 - parity, core, d, at, size)
+                got = send(block, block, other, up_z if d == 0 else down_z)
+                z_got.setdefault((r, d), []).append((at, size, got))
+            pass_on(r, parity if shared else None, d, at, size)
 
     def on_z(r, d):
-        z_got[r, d]()
-        block = piece(panel.at[r], 1 - parity, core, d)
-        theirs = piece(panel.at[r], 1 - parity, 1 - core, d)
-        pass_z[r, d] = send(block, block, theirs, sibling)
+        for at, size, got in z_got[r, d]:
+            got()
+            pass_on(r, 1 - parity, d, at, size)
 
     def slot_done(r):
-        for d in range(2):
-            pass_x[r, d]()
-            pass_z[r, d]()
+        for got in passed[r]:
+            got()
+
+    own_x(True, 0, fine, 3)
+    own_x(True, 1, fine, 1)
+    own_x(True, 1, coarse, 3)
+    own_x(True, 0, coarse, 1)
 
     def part_of(ref, i):
         return ref.at[pl.ds(pl.multiple_of(i * 64, 64), 64)]
 
     def spread(local, got):
         waits = []
-        for o in range(1, 8):
+        for o in (4, 5, 3, 6, 2, 7, 1):
             to, source = lax.rem(member + o, 8), lax.rem(member + 8 - o, 8)
             waits.append(
                 send(part_of(local, to), part_of(got, member), part_of(got, source), mate(to))
@@ -157,7 +172,7 @@
             out[i * 64 : i * 64 + 64] = running.astype(BF)
             running = running + got[i * 64 : i * 64 + 64].astype(F32)
         waits = []
-        for o in range(1, 8):
+        for o in (4, 5, 3, 6, 2, 7, 1):
             to, source = lax.rem(member + o, 8), lax.rem(member + 8 - o, 8)
             waits.append(
                 send(part_of(out, to), part_of(state, member), part_of(state, source), mate(to))
@@ -186,15 +201,26 @@
     for h in range(heads):
         scores = (dot(head(q_ref, h), head(k_ref, h), 1, 1) * causal).astype(BF)
         attn32[:, h * DH : (h + 1) * DH] = dot(scores, head(v_ref, h), 1, 0)
-
-    kv_waits = totals(kv_waits, got_kv, tot_kv, far_kv)
     load_w.wait()
     load_go[0].wait()
+
+    on_x(3, True, 0)
+    on_x(1, True, 1)
+    kv_waits = totals(kv_waits, got_kv, tot_kv, far_kv)
     grad_acc[...] = dot(go[0], panel[0], 1, 1)
-
+    on_x(3, True, 1)
+    on_x(1, True, 0)
+    for d, r in ((0, 3), (1, 1), (1, 3), (0, 1)):
+        own_x(False, d, whole, r)
+    on_z(3, 0)
+    on_z(1, 1)
     kv_waits = scan(kv_waits, got_kv, far_kv, out_kv, prefix, False)
-    on_x(3, 0)
-    on_x(1, 1)
+    on_x(2, True, 0)
+    on_x(2, True, 1)
+    on_z(3, 1)
+    on_z(1, 0)
+    on_x(3, False, 0)
+    on_x(1, False, 1)
     for wait in kv_waits:
         wait()
     for h in range(heads):
@@ -209,22 +235,19 @@
                 attn16[...], panel[r, :, i * half : (i + 1) * half], 1, 0
             ).astype(BF)
 
+    on_x(3, False, 1)
+    on_x(1, False, 0)
     project(0)
-    on_x(3, 1)
-    on_x(1, 0)
-    on_z(3, 0)
-    on_z(1, 1)
-    on_x(2, 0)
-    on_x(2, 1)
-    on_z(3, 1)
-    on_z(1, 0)
+    on_z(2, 0)
+    on_z(2, 1)
     for r in (3, 1):
         slot_done(r)
         load_go[r].wait()
         grad_acc[...] += dot(go[r], panel[r], 1, 1)
+        if r == 3:
+            on_x(2, False, 0)
+            on_x(2, False, 1)
         project(r)
-    on_z(2, 0)
-    on_z(2, 1)
     slot_done(2)
     load_go[2].wait()
 
@@ -256,28 +279,32 @@
     for h in range(heads):
         local_qd[h * DH : (h + 1) * DH, :] = dot(head(q_ref, h), g_heads[h], 0, 0).astype(BF)
     qd_waits = spread(local_qd, got_qd)
-    y_step(2)
-    qd_waits = totals(qd_waits, got_qd, tot_qd, far_qd)
-    y_step(3)
     for h in range(heads):
         own = slice(h * DH, (h + 1) * DH)
         d_scores = (dot(g_heads[h], head(v_ref, h), 1, 1) * causal).astype(BF)
         total = dot(d_scores, head(k_ref, h), 1, 0) + dot(g_heads[h], state_of(prefix, h), 1, 1)
         dq_ref[0, :, own] = (factor * total).astype(BF)
+    y_step(2)
+    qd_waits = totals(qd_waits, got_qd, tot_qd, far_qd)
+    y_step(3)
+    for h in range(heads):
+        own = slice(h * DH, (h + 1) * DH)
+        d_scores = (dot(head(v_ref, h), g_heads[h], 1, 1) * causal_t).astype(BF)
+        attn32[:, own] = dot(d_scores, head(q_ref, h), 1, 0)
+        scores = (dot(head(k_ref, h), head(q_ref, h), 1, 1) * causal_t).astype(BF)
+        grad_acc[:, own] = dot(scores, g_heads[h], 1, 0)
+    y_step(4)
     qd_waits = scan(qd_waits, got_qd, far_qd, out_qd, suffix, True)
-    y_step(4)
+    y_step(5)
+    y_step(6)
     for wait in qd_waits:
         wait()
     for h in range(heads):
         own = slice(h * DH, (h + 1) * DH)
-        d_scores = (dot(head(v_ref, h), g_heads[h], 1, 1) * causal_t).astype(BF)
-        total = dot(d_scores, head(q_ref, h), 1, 0) + dot(head(v_ref, h), state_of(suffix, h), 1, 1)
+        total = attn32[:, own] + dot(head(v_ref, h), state_of(suffix, h), 1, 1)
         dk_ref[0, :, own] = (factor * total).astype(BF)
-        scores = (dot(head(k_ref, h), head(q_ref, h), 1, 1) * causal_t).astype(BF)
-        total = dot(scores, g_heads[h], 1, 0) + dot(head(k_ref, h), state_of(suffix, h), 1, 0)
+        total = grad_acc[:, own] + dot(head(k_ref, h), state_of(suffix, h), 1, 0)
         dv_ref[0, :, own] = (factor * total).astype(BF)
-    y_step(5)
-    y_step(6)
     for which in range(2):
         up, down = 6 - which, 5 + which
         y_got[0][up]()
@@ -287,6 +314,15 @@
         att_ref[0, :, which * half : (which + 1) * half] = total.astype(BF)
     for copy in sent:
         copy.wait_send()
+
+
+def hand_over(*refs):
+    n = len(refs) // 2
+    copies = [pltpu.make_async_copy(refs[i], refs[n + i], refs[-1].at[i]) for i in range(n)]
+    for copy in copies:
+        copy.start()
+    for copy in copies:
+        copy.wait()
 
 
 def solution(mesh):
@@ -303,14 +339,15 @@
         state = pltpu.VMEM((states, DH), BF)
         total = pltpu.VMEM((states // 8, DH), BF)
         far = pltpu.VMEM((2, states // 8, DH), BF)
-        return pl.pallas_call(
+        results = (
+            jax.ShapeDtypeStruct((1, rows, n_x * wide // n_y), BF),
+            head_out,
+            head_out,
+            head_out,
+        )
+        ready = pl.pallas_call(
             functools.partial(kernel, sizes),
-            out_shape=(
-                jax.ShapeDtypeStruct((1, rows, n_x * wide // n_y), BF),
-                head_out,
-                head_out,
-                head_out,
-            ),
+            out_shape=results,
             in_specs=[pl.BlockSpec(memory_space=pl.ANY)] * 5,
             out_specs=[pl.BlockSpec(memory_space=pltpu.VMEM)] * 4,
             scratch_shapes=[
@@ -326,14 +363,21 @@
                 pltpu.VMEM((14, rows, half), BF),
                 state, state, state, state, total, total, far, far,
                 state, state, state, state,
-                pltpu.SemaphoreType.DMA((70,)),
-                pltpu.SemaphoreType.DMA((70,)),
+                pltpu.SemaphoreType.DMA((98,)),
+                pltpu.SemaphoreType.DMA((98,)),
                 pltpu.SemaphoreType.DMA((8,)),
             ],
             compiler_params=pltpu.CompilerParams(
                 collective_id=0, has_side_effects=True, vmem_limit_bytes=56 << 20
             ),
         )(q, k, v, w, go)
+        return pl.pallas_call(
+            hand_over,
+            out_shape=results,
+            in_specs=[pl.BlockSpec(memory_space=pl.ANY)] * 4,
+            out_specs=[pl.BlockSpec(memory_space=pl.ANY)] * 4,
+            scratch_shapes=[pltpu.SemaphoreType.DMA((4,))],
+        )(*ready)
 
     rows_spec = P("dp", "context", "tensor")
     return jax.shard_map(

time: 76.9 us -> 82 us (1.066)
  Pallas kernels: 69.7 us -> 81.2 us
  local copies, waits for them, and re-layouts: 6.32 us -> 0 us
    pallas_call x1 -> x2, Pallas kernels: 69.7 us -> 81.2 us  [the longest x1 62.2 us: shards(): pl.pallas_call(functools.partial(kernel, sizes), out_shape=results, in_sp...]
    unnamed x4 -> x0, local copies, waits for them, and re-layouts: 6.32 us -> none
where the time goes in v2:
time: 82 us; the launch traced here: 81.8 us
  Pallas kernels  81.2 us (99%)
    pallas_call x1, Pallas kernels, shards(): pl.pallas_call(functools.partial(kernel, sizes), out_shape=results, in_sp...  62.2 us
    pallas_call x1, Pallas kernels, shards(): pl.pallas_call(hand_over, out_shape=results, in_specs=[pl.BlockSpec(memor...  19 us

profile of v2, /device:TPU:1, one launch (start us, length us, event | category | flops | bytes accessed | tf_op | source)
XLA Modules:
  0.0 81.8 jit_solution(11698784118329000129)
XLA Ops:
  0.6 62.2 %shard_map.84 = (bf16[1,128,768]{2,1,0:T(8,128)(2,1)}, bf16[1,128,512]{2,1,0:T(8,128)(2,1)}, bf16[1,128,512]{2,1,0:T(8,128)(2,1)}, bf16[1,128,512]{2,1,0:T(8,128)(2,1)}) custom-call(bf16[1,128,512]{2,1,0:T(8,128)(2,1)} %q_hbm.1, bf16[1,128,512]{2,1,0:T(8,128)(2,1)} %k_hbm.1, bf16[1,128,512]{2,1,0:T(8,128)(2,1)} %v_hbm.1, bf16[512,1536]{1,0:T(8,128)(2,1)} %w_hbm.1, ...), custom_call_target="tpu_custom_call" | custom-call | tf_op jit(solution)/shard_map/pallas_call | solution.py:348
  62.8 19.0 %shard_map.85 = (bf16[1,128,768]{2,1,0:T(8,128)(2,1)}, bf16[1,128,512]{2,1,0:T(8,128)(2,1)}, bf16[1,128,512]{2,1,0:T(8,128)(2,1)}, bf16[1,128,512]{2,1,0:T(8,128)(2,1)}) custom-call(bf16[1,128,768]{2,1,0:T(8,128)(2,1)} %get-tuple-element.8.refs_0_, bf16[1,128,512]{2,1,0:T(8,128)(2,1)} %get-tuple-element.9.refs_1_, ...), custom_call_target="tpu_custom_call" | custom-call | tf_op jit(solution)/shard_map/pallas_call | solution.py:374

commit v3 on v2

--- a/solution.py
+++ b/solution.py
@@ -348,7 +348,7 @@
         ready = pl.pallas_call(
             functools.partial(kernel, sizes),
             out_shape=results,
-            in_specs=[pl.BlockSpec(memory_space=pl.ANY)] * 5,
+            in_specs=[pl.BlockSpec(memory_space=pltpu.HBM)] * 5,
             out_specs=[pl.BlockSpec(memory_space=pltpu.VMEM)] * 4,
             scratch_shapes=[
                 pltpu.VMEM((rows, width), BF),
@@ -368,7 +368,7 @@
                 pltpu.SemaphoreType.DMA((8,)),
             ],
             compiler_params=pltpu.CompilerParams(
-                collective_id=0, has_side_effects=True, vmem_limit_bytes=56 << 20
+                collective_id=0, has_side_effects=True, vmem_limit_bytes=54784 << 10
             ),
         )(q, k, v, w, go)
         return pl.pallas_call(
@@ -377,6 +377,7 @@
             in_specs=[pl.BlockSpec(memory_space=pl.ANY)] * 4,
             out_specs=[pl.BlockSpec(memory_space=pl.ANY)] * 4,
             scratch_shapes=[pltpu.SemaphoreType.DMA((4,))],
+            compiler_params=pltpu.CompilerParams(vmem_limit_bytes=1 << 20),
         )(*ready)
 
     rows_spec = P("dp", "context", "tensor")

time: 82 us -> 64.5 us (0.79)
  Pallas kernels: 81.2 us -> 62.8 us
  local copies, waits for them, and re-layouts: 0 us -> 0.92 us
    pallas_call x1, Pallas kernels: 19 us -> 0.84 us  [shards(): pl.pallas_call(hand_over, out_shape=results, in_specs=[pl.BlockSpec(memor...]
    unnamed x0 -> x2, local copies, waits for them, and re-layouts: none -> 0.92 us
where the time goes in v3:
time: 64.5 us; the launch traced here: 64.4 us
  Pallas kernels  62.8 us (97%)
  local copies, waits for them, and re-layouts  0.92 us (1%)
  between operations  0.65 us (1%)
    pallas_call x1, Pallas kernels, shards(): pl.pallas_call(functools.partial(kernel, sizes), out_shape=results, in_sp...  62 us

profile of v3, /device:TPU:1, one launch (start us, length us, event | category | flops | bytes accessed | tf_op | source)
XLA Modules:
  0.0 64.4 jit_solution(12501840825832914689)
XLA Ops:
  0.6 62.0 %shard_map.84 = (bf16[1,128,768]{2,1,0:T(8,128)(2,1)}, bf16[1,128,512]{2,1,0:T(8,128)(2,1)S(1)}, bf16[1,128,512]{2,1,0:T(8,128)(2,1)S(1)}, bf16[1,128,512]{2,1,0:T(8,128)(2,1)S(1)}) custom-call(bf16[1,128,512]{2,1,0:T(8,128)(2,1)} %q_hbm.1, bf16[1,128,512]{2,1,0:T(8,128)(2,1)} %k_hbm.1, bf16[1,128,512]{2,1,0:T(8,128)(2,1)} %v_hbm.1, ...), custom_call_target="tpu_custom_call" | custom-call | tf_op jit(solution)/shard_map/pallas_call | solution.py:348
  62.6 0.0 copy-start
  62.6 0.9 %copy-done = bf16[1,128,768]{2,1,0:T(8,128)(2,1)S(1)} copy-done((bf16[1,128,768]{2,1,0:T(8,128)(2,1)S(1)}, bf16[1,128,768]{2,1,0:T(8,128)(2,1)}, u32[]{:S(2)}) %copy-start) | copy-done | bytes 196632
  63.5 0.8 %shard_map.85 = (bf16[1,128,768]{2,1,0:T(8,128)(2,1)}, bf16[1,128,512]{2,1,0:T(8,128)(2,1)}, bf16[1,128,512]{2,1,0:T(8,128)(2,1)}, bf16[1,128,512]{2,1,0:T(8,128)(2,1)}) custom-call(bf16[1,128,768]{2,1,0:T(8,128)(2,1)S(1)} %copy-done, bf16[1,128,512]{2,1,0:T(8,128)(2,1)S(1)} %get-tuple-element.9.refs_1_, bf16[1,128,512]{2,1,0:T(8,128)(2,1)S(1)} %get-tuple-element.10.refs_2_, ...), custom_call_target="tpu_custom_call" | custom-call | tf_op jit(solution)/shard_map/pallas_call | solution.py:374
Async XLA Ops:
  62.6 0.9 %copy-start = (bf16[1,128,768]{2,1,0:T(8,128)(2,1)S(1)}, bf16[1,128,768]{2,1,0:T(8,128)(2,1)}, u32[]{:S(2)}) copy-start(bf16[1,128,768]{2,1,0:T(8,128)(2,1)} %get-tuple-element.8.refs_0_) | copy-start | bytes 589828

commit v4 on v3

--- a/solution.py
+++ b/solution.py
@@ -21,7 +21,7 @@
     sizes, q_hbm, k_hbm, v_hbm, w_hbm, go_hbm, att_ref, dq_ref, dk_ref, dv_ref,
     q_ref, k_ref, v_ref, panel, go, grad_acc, attn32, attn16, part, y_in,
     local_kv, local_qd, got_kv, got_qd, tot_kv, tot_qd, far_kv, far_qd,
-    out_kv, out_qd, prefix, suffix, send_sem, recv_sem, load_sem,
+    out_kv, out_qd, prefix, suffix, send_sem, recv_sem, load_sem, gate,
 ):
     n_ctx, n_x, n_y, factor = sizes
     rows, width = q_ref.shape
@@ -47,7 +47,6 @@
     barrier = pltpu.get_barrier_semaphore()
     peers = [right_x, left_x, up_y, down_y, up_z, down_z]
     peers += [mate(lax.rem(member + o, 8)) for o in range(1, 8)]
-    peers += [at_ctx(c + 8 * o) for o in range(1, n_groups)]
     for peer in peers:
         pl.semaphore_signal(barrier, inc=1, device_id=peer, device_id_type=MESH)
 
@@ -68,6 +67,33 @@
         columns = pl.ds(pl.multiple_of(lax.rem(x + r, n_x) * wide, wide), wide)
         load_go.append(load(go_hbm.at[0, :, columns], go.at[r]))
     pl.semaphore_wait(barrier, len(peers))
+
+    def signal(i, device):
+        pl.semaphore_signal(gate.at[i], inc=1, device_id=device, device_id_type=MESH)
+
+    @pl.when(member == 0)
+    def _():
+        signal(0, down_z)
+
+    @pl.when(member == 6)
+    def _():
+        signal(0, up_z)
+
+    def greet():
+        for i, end in ((1, 0), (2, 6)):
+
+            @pl.when(member == end)
+            def _():
+                pl.semaphore_wait(gate.at[0], 1)
+                for o in range(1, 8):
+                    signal(i, mate(lax.rem(member + o, 8)))
+
+    def greeted():
+        for i, end in ((1, 0), (2, 6)):
+
+            @pl.when(member != end)
+            def _():
+                pl.semaphore_wait(gate.at[i], 1)
 
     sent = []
 
@@ -201,11 +227,13 @@
     for h in range(heads):
         scores = (dot(head(q_ref, h), head(k_ref, h), 1, 1) * causal).astype(BF)
         attn32[:, h * DH : (h + 1) * DH] = dot(scores, head(v_ref, h), 1, 0)
+    greet()
     load_w.wait()
     load_go[0].wait()
 
     on_x(3, True, 0)
     on_x(1, True, 1)
+    greeted()
     kv_waits = totals(kv_waits, got_kv, tot_kv, far_kv)
     grad_acc[...] = dot(go[0], panel[0], 1, 1)
     on_x(3, True, 1)
@@ -285,8 +313,8 @@
         total = dot(d_scores, head(k_ref, h), 1, 0) + dot(g_heads[h], state_of(prefix, h), 1, 1)
         dq_ref[0, :, own] = (factor * total).astype(BF)
     y_step(2)
+    y_step(3)
     qd_waits = totals(qd_waits, got_qd, tot_qd, far_qd)
-    y_step(3)
     for h in range(heads):
         own = slice(h * DH, (h + 1) * DH)
         d_scores = (dot(head(v_ref, h), g_heads[h], 1, 1) * causal_t).astype(BF)
@@ -294,8 +322,8 @@
         scores = (dot(head(k_ref, h), head(q_ref, h), 1, 1) * causal_t).astype(BF)
         grad_acc[:, own] = dot(scores, g_heads[h], 1, 0)
     y_step(4)
+    y_step(5)
     qd_waits = scan(qd_waits, got_qd, far_qd, out_qd, suffix, True)
-    y_step(5)
     y_step(6)
     for wait in qd_waits:
         wait()
@@ -366,6 +394,7 @@
                 pltpu.SemaphoreType.DMA((98,)),
                 pltpu.SemaphoreType.DMA((98,)),
                 pltpu.SemaphoreType.DMA((8,)),
+                pltpu.SemaphoreType.REGULAR((3,)),
             ],
             compiler_params=pltpu.CompilerParams(
                 collective_id=0, has_side_effects=True, vmem_limit_bytes=54784 << 10

time: 64.5 us -> 61.5 us (0.953)
  Pallas kernels: 62.8 us -> 59.7 us
    pallas_call x1, Pallas kernels: 62 us -> 58.9 us  [shards(): pl.pallas_call(functools.partial(kernel, sizes), out_shape=results, in_sp...]
where the time goes in v4:
time: 61.5 us; the launch traced here: 61.3 us
  Pallas kernels  59.7 us (97%)
  local copies, waits for them, and re-layouts  0.92 us (1%)
  between operations  0.65 us (1%)
    pallas_call x1, Pallas kernels, shards(): pl.pallas_call(functools.partial(kernel, sizes), out_shape=results, in_sp...  58.9 us

profile of v4, /device:TPU:1, one launch (start us, length us, event | category | flops | bytes accessed | tf_op | source)
XLA Modules:
  0.0 61.3 jit_solution(1339091528627244701)
XLA Ops:
  0.6 58.9 %shard_map.84 = (bf16[1,128,768]{2,1,0:T(8,128)(2,1)}, bf16[1,128,512]{2,1,0:T(8,128)(2,1)S(1)}, bf16[1,128,512]{2,1,0:T(8,128)(2,1)S(1)}, bf16[1,128,512]{2,1,0:T(8,128)(2,1)S(1)}) custom-call(bf16[1,128,512]{2,1,0:T(8,128)(2,1)} %q_hbm.1, bf16[1,128,512]{2,1,0:T(8,128)(2,1)} %k_hbm.1, bf16[1,128,512]{2,1,0:T(8,128)(2,1)} %v_hbm.1, ...), custom_call_target="tpu_custom_call" | custom-call | tf_op jit(solution)/shard_map/pallas_call | solution.py:376
  59.5 0.0 copy-start
  59.5 0.9 %copy-done = bf16[1,128,768]{2,1,0:T(8,128)(2,1)S(1)} copy-done((bf16[1,128,768]{2,1,0:T(8,128)(2,1)S(1)}, bf16[1,128,768]{2,1,0:T(8,128)(2,1)}, u32[]{:S(2)}) %copy-start) | copy-done | bytes 196632
  60.5 0.8 %shard_map.85 = (bf16[1,128,768]{2,1,0:T(8,128)(2,1)}, bf16[1,128,512]{2,1,0:T(8,128)(2,1)}, bf16[1,128,512]{2,1,0:T(8,128)(2,1)}, bf16[1,128,512]{2,1,0:T(8,128)(2,1)}) custom-call(bf16[1,128,768]{2,1,0:T(8,128)(2,1)S(1)} %copy-done, bf16[1,128,512]{2,1,0:T(8,128)(2,1)S(1)} %get-tuple-element.9.refs_1_, bf16[1,128,512]{2,1,0:T(8,128)(2,1)S(1)} %get-tuple-element.10.refs_2_, ...), custom_call_target="tpu_custom_call" | custom-call | tf_op jit(solution)/shard_map/pallas_call | solution.py:403
Async XLA Ops:
  59.5 0.9 %copy-start = (bf16[1,128,768]{2,1,0:T(8,128)(2,1)S(1)}, bf16[1,128,768]{2,1,0:T(8,128)(2,1)}, u32[]{:S(2)}) copy-start(bf16[1,128,768]{2,1,0:T(8,128)(2,1)} %get-tuple-element.8.refs_0_) | copy-start | bytes 589828

commit v5 on v4

--- a/solution.py
+++ b/solution.py
@@ -268,14 +268,12 @@
     project(0)
     on_z(2, 0)
     on_z(2, 1)
-    for r in (3, 1):
-        slot_done(r)
-        load_go[r].wait()
-        grad_acc[...] += dot(go[r], panel[r], 1, 1)
-        if r == 3:
-            on_x(2, False, 0)
-            on_x(2, False, 1)
-        project(r)
+    slot_done(3)
+    project(3)
+    on_x(2, False, 0)
+    on_x(2, False, 1)
+    slot_done(1)
+    project(1)
     slot_done(2)
     load_go[2].wait()
 
@@ -302,6 +300,9 @@
     project(2)
     y_step(0)
     y_step(1)
+    for r in (3, 1):
+        load_go[r].wait()
+        grad_acc[...] += dot(go[r], panel[r], 1, 1)
     grads = (grad_acc[...] + dot(go[2], panel[2], 1, 1)).astype(BF)
     g_heads = [grads[:, h * DH : (h + 1) * DH] for h in range(heads)]
     for h in range(heads):

time: 61.5 us -> 61.5 us (level)
  no operation moved by 1% of the time
where the time goes in v5:
time: 61.5 us; the launch traced here: 61.1 us
  Pallas kernels  59.5 us (97%)
  local copies, waits for them, and re-layouts  0.92 us (1%)
  between operations  0.65 us (1%)
    pallas_call x1, Pallas kernels, shards(): pl.pallas_call(functools.partial(kernel, sizes), out_shape=results, in_sp...  58.7 us

profile of v5, /device:TPU:1, one launch (start us, length us, event | category | flops | bytes accessed | tf_op | source)
XLA Modules:
  0.0 61.1 jit_solution(3925544343874482593)
XLA Ops:
  0.6 58.7 %shard_map.84 = (bf16[1,128,768]{2,1,0:T(8,128)(2,1)}, bf16[1,128,512]{2,1,0:T(8,128)(2,1)S(1)}, bf16[1,128,512]{2,1,0:T(8,128)(2,1)S(1)}, bf16[1,128,512]{2,1,0:T(8,128)(2,1)S(1)}) custom-call(bf16[1,128,512]{2,1,0:T(8,128)(2,1)} %q_hbm.1, bf16[1,128,512]{2,1,0:T(8,128)(2,1)} %k_hbm.1, bf16[1,128,512]{2,1,0:T(8,128)(2,1)} %v_hbm.1, ...), custom_call_target="tpu_custom_call" | custom-call | tf_op jit(solution)/shard_map/pallas_call | solution.py:377
  59.3 0.0 copy-start
  59.3 0.9 %copy-done = bf16[1,128,768]{2,1,0:T(8,128)(2,1)S(1)} copy-done((bf16[1,128,768]{2,1,0:T(8,128)(2,1)S(1)}, bf16[1,128,768]{2,1,0:T(8,128)(2,1)}, u32[]{:S(2)}) %copy-start) | copy-done | bytes 196632
  60.3 0.8 %shard_map.85 = (bf16[1,128,768]{2,1,0:T(8,128)(2,1)}, bf16[1,128,512]{2,1,0:T(8,128)(2,1)}, bf16[1,128,512]{2,1,0:T(8,128)(2,1)}, bf16[1,128,512]{2,1,0:T(8,128)(2,1)}) custom-call(bf16[1,128,768]{2,1,0:T(8,128)(2,1)S(1)} %copy-done, bf16[1,128,512]{2,1,0:T(8,128)(2,1)S(1)} %get-tuple-element.9.refs_1_, bf16[1,128,512]{2,1,0:T(8,128)(2,1)S(1)} %get-tuple-element.10.refs_2_, ...), custom_call_target="tpu_custom_call" | custom-call | tf_op jit(solution)/shard_map/pallas_call | solution.py:404
Async XLA Ops:
  59.3 0.9 %copy-start = (bf16[1,128,768]{2,1,0:T(8,128)(2,1)S(1)}, bf16[1,128,768]{2,1,0:T(8,128)(2,1)}, u32[]{:S(2)}) copy-start(bf16[1,128,768]{2,1,0:T(8,128)(2,1)} %get-tuple-element.8.refs_0_) | copy-start | bytes 589828

commit v6 on v4

--- a/solution.py
+++ b/solution.py
@@ -60,12 +60,6 @@
 
     load_k = load(k_hbm.at[0], k_ref)
     load_v = load(v_hbm.at[0], v_ref)
-    load_q = load(q_hbm.at[0], q_ref)
-    load_w = load(w_hbm, panel.at[0])
-    load_go = []
-    for r in range(n_x):
-        columns = pl.ds(pl.multiple_of(lax.rem(x + r, n_x) * wide, wide), wide)
-        load_go.append(load(go_hbm.at[0, :, columns], go.at[r]))
     pl.semaphore_wait(barrier, len(peers))
 
     def signal(i, device):
@@ -164,6 +158,13 @@
     own_x(True, 1, fine, 1)
     own_x(True, 1, coarse, 3)
     own_x(True, 0, coarse, 1)
+
+    load_q = load(q_hbm.at[0], q_ref)
+    load_w = load(w_hbm, panel.at[0])
+    load_go = []
+    for r in range(n_x):
+        columns = pl.ds(pl.multiple_of(lax.rem(x + r, n_x) * wide, wide), wide)
+        load_go.append(load(go_hbm.at[0, :, columns], go.at[r]))
 
     def part_of(ref, i):
         return ref.at[pl.ds(pl.multiple_of(i * 64, 64), 64)]

time: 61.5 us -> 61.5 us (level)
  no operation moved by 1% of the time
where the time goes in v6:
time: 61.5 us; the launch traced here: 61.3 us
  Pallas kernels  59.7 us (97%)
  local copies, waits for them, and re-layouts  0.92 us (1%)
  between operations  0.65 us (1%)
    pallas_call x1, Pallas kernels, shards(): pl.pallas_call(functools.partial(kernel, sizes), out_shape=results, in_sp...  58.9 us

profile of v6, /device:TPU:1, one launch (start us, length us, event | category | flops | bytes accessed | tf_op | source)
XLA Modules:
  0.0 61.3 jit_solution(14230078107327948909)
XLA Ops:
  0.6 58.9 %shard_map.84 = (bf16[1,128,768]{2,1,0:T(8,128)(2,1)}, bf16[1,128,512]{2,1,0:T(8,128)(2,1)S(1)}, bf16[1,128,512]{2,1,0:T(8,128)(2,1)S(1)}, bf16[1,128,512]{2,1,0:T(8,128)(2,1)S(1)}) custom-call(bf16[1,128,512]{2,1,0:T(8,128)(2,1)} %q_hbm.1, bf16[1,128,512]{2,1,0:T(8,128)(2,1)} %k_hbm.1, bf16[1,128,512]{2,1,0:T(8,128)(2,1)} %v_hbm.1, ...), custom_call_target="tpu_custom_call" | custom-call | tf_op jit(solution)/shard_map/pallas_call | solution.py:377
  59.5 0.0 copy-start
  59.5 0.9 %copy-done = bf16[1,128,768]{2,1,0:T(8,128)(2,1)S(1)} copy-done((bf16[1,128,768]{2,1,0:T(8,128)(2,1)S(1)}, bf16[1,128,768]{2,1,0:T(8,128)(2,1)}, u32[]{:S(2)}) %copy-start) | copy-done | bytes 196632
  60.5 0.8 %shard_map.85 = (bf16[1,128,768]{2,1,0:T(8,128)(2,1)}, bf16[1,128,512]{2,1,0:T(8,128)(2,1)}, bf16[1,128,512]{2,1,0:T(8,128)(2,1)}, bf16[1,128,512]{2,1,0:T(8,128)(2,1)}) custom-call(bf16[1,128,768]{2,1,0:T(8,128)(2,1)S(1)} %copy-done, bf16[1,128,512]{2,1,0:T(8,128)(2,1)S(1)} %get-tuple-element.9.refs_1_, bf16[1,128,512]{2,1,0:T(8,128)(2,1)S(1)} %get-tuple-element.10.refs_2_, ...), custom_call_target="tpu_custom_call" | custom-call | tf_op jit(solution)/shard_map/pallas_call | solution.py:404
Async XLA Ops:
  59.5 0.9 %copy-start = (bf16[1,128,768]{2,1,0:T(8,128)(2,1)S(1)}, bf16[1,128,768]{2,1,0:T(8,128)(2,1)}, u32[]{:S(2)}) copy-start(bf16[1,128,768]{2,1,0:T(8,128)(2,1)} %get-tuple-element.8.refs_0_) | copy-start | bytes 589828
